TPU v7x, 32 devices: a whole 2x2x4 slice. The times are simulated.
32 devices in a mesh: batch: 32 (over z, y, x, core).
Axes of the slice: x: 2, y: 2, z: 4, core: 2. Of those that a mesh axis runs over, the one named last changes fastest.
Arguments:
- image_emb: bfloat16 [24576, 1152], P('batch'), may hold values from -300 to 300, as said below
- text_emb: bfloat16 [24576, 1152], P('batch'), may hold values from -300 to 300, as said below
- logit_scale: float32 [1], replicated, may hold values from 8 to 12
- logit_bias: float32 [1], replicated, may hold values from -3 to -1
Outputs:
- image_grad: bfloat16 [24576, 1152], P('batch')
- text_grad: bfloat16 [24576, 1152], P('batch')
Inputs may be any that keep to these rules, and one draw needn't show every extreme that they name: `image_emb`: finite values, rows of differing magnitude. `text_emb`: finite values, rows of differing magnitude.
All inputs are finite; a program needn't handle non-finite values.
Results may differ from a plain program's by a relative error of at most 0.0034.
Values may be sent and summed in bfloat16 or wider, within the bound.
No kernel may reach another device: no remote copies, remote signals or barrier semaphores. Data moves between devices by JAX's collectives and lax.ppermute only.
A program may use at most 64 MiB of HBM per device.

v0:
```python
import jax
import jax.numpy as jnp
from jax import lax
from jax.sharding import PartitionSpec as P

STEPS = 4


EPS = 1e-06


def from_behind(block, axis, distance):
    devices = range(lax.axis_size(axis))
    route = [((i - distance) % len(devices), i) for i in devices]
    return lax.ppermute(block, axis, route)


def unit_rows(raw):
    wide = raw.astype(jnp.float32)
    inv = lax.rsqrt(jnp.sum(wide * wide, axis=-1, keepdims=True) + EPS)
    return (wide * inv, inv)


def project_back(unit, inv, acc):
    along = jnp.sum(unit * acc, axis=-1, keepdims=True)
    return (inv * (acc - unit * along)).astype(jnp.bfloat16)


def tile_coef(image_block, text_block, scale, bias, label):
    logits = scale * jnp.dot(image_block, text_block.T, preferred_element_type=jnp.float32) + bias
    coef = jax.nn.sigmoid(logits)
    if label is not None:
        coef = coef - label
    return coef.astype(jnp.bfloat16)


def image_side(coef, text_block):
    return jnp.dot(coef, text_block, preferred_element_type=jnp.float32)


def text_side(coef, image_block):
    return lax.dot_general(
        coef, image_block, (((0,), (0,)), ((), ())), preferred_element_type=jnp.float32
    )


def shards(image_emb, text_emb, logit_scale, logit_bias):
    scale = logit_scale[0]
    bias = logit_bias[0]
    rows = image_emb.shape[0]
    image_unit, image_inv = unit_rows(image_emb)
    text_unit, text_inv = unit_rows(text_emb)
    image_hat = image_unit.astype(jnp.bfloat16)
    text_hat = text_unit.astype(jnp.bfloat16)
    label = jnp.eye(rows, dtype=jnp.float32)
    own_coef = tile_coef(image_hat, text_hat, scale, bias, label)
    image_acc = image_side(own_coef, text_hat)
    own_text = text_side(own_coef, image_hat)
    moving = text_hat
    carried = own_text
    for step in range(STEPS):
        moving = from_behind(moving, "batch", 1)
        carried = from_behind(carried, "batch", 1)
        coef = tile_coef(image_hat, moving, scale, bias, None)
        image_acc = image_acc + image_side(coef, moving)
        carried = carried + text_side(coef, image_hat)
    text_acc = from_behind(carried, "batch", -STEPS)
    image_grad = project_back(image_unit, image_inv, scale * image_acc)
    text_grad = project_back(text_unit, text_inv, scale * text_acc)
    return (image_grad, text_grad)


def solution(mesh):
    placed = (P("batch", None), P("batch", None), P(), P())
    return jax.shard_map(
        shards,
        mesh=mesh,
        in_specs=placed,
        out_specs=(P("batch", None), P("batch", None)),
        check_vma=False,
    )
```

profile of v0, /device:TPU:0, one launch (start us, length us, event | category | flops | bytes accessed | tf_op | source)
XLA Modules:
  0.0 354.7 jit_solution(13530772517534941369)
XLA Ops:
  0.6 0.0 copy-start
  0.6 2.0 fusion.11
  2.7 0.0 copy-done
  2.7 0.0 copy-start.1
  2.7 0.4 fusion.16
  3.1 0.4 fusion.2
  4.8 0.0 copy-done.1
  4.8 2.0 subtract_convert_fusion
  6.8 1.9 fusion.24
  8.7 0.5 collective-permute-start.4
  9.2 2.6 collective-permute-start
  11.8 61.5 %collective-permute-done = bf16[768,1152]{1,0:T(8,128)(2,1)S(1)} collective-permute-done((bf16[768,1152]{1,0:T(8,128)(2,1)S(1)}, bf16[768,1152]{1,0:T(8,128)(2,1)S(1)}, u32[]{:S(2)}, u32[]{:S(2)}) %collective-permute-start) | collective-permute-done | bytes 1769504 | tf_op jit(solution)/shard_map/ppermute | solution.py:15
  73.2 2.0 divide_convert_fusion.3
  75.2 0.0 collective-permute-done.4
  75.2 1.9 convolution_add_fusion
  77.1 0.1 collective-permute-start.5
  77.2 0.1 collective-permute-start.1
  77.3 63.4 %collective-permute-done.1 = bf16[768,1152]{1,0:T(8,128)(2,1)S(1)} collective-permute-done((bf16[768,1152]{1,0:T(8,128)(2,1)S(1)}, bf16[768,1152]{1,0:T(8,128)(2,1)S(1)}, u32[]{:S(2)}, u32[]{:S(2)}) %collective-permute-start.1) | collective-permute-done | bytes 1769504 | tf_op jit(solution)/shard_map/ppermute | solution.py:15
  140.7 2.0 divide_convert_fusion.2
  142.6 1.9 fusion.21
  144.5 0.0 collective-permute-done.5
  144.5 0.4 add.95
  144.9 0.1 collective-permute-start.6
  145.0 0.2 collective-permute-start.2
  145.2 63.2 %collective-permute-done.2 = bf16[768,1152]{1,0:T(8,128)(2,1)S(1)} collective-permute-done((bf16[768,1152]{1,0:T(8,128)(2,1)S(1)}, bf16[768,1152]{1,0:T(8,128)(2,1)S(1)}, u32[]{:S(2)}, u32[]{:S(2)}) %collective-permute-start.2) | collective-permute-done | bytes 1769504 | tf_op jit(solution)/shard_map/ppermute | solution.py:15
  208.4 2.0 divide_convert_fusion.1
  210.4 1.9 fusion.19
  212.3 0.0 collective-permute-done.6
  212.3 0.4 add.96
  212.6 0.1 collective-permute-start.7
  212.7 0.1 collective-permute-start.3
  212.8 63.5 %collective-permute-done.3 = bf16[768,1152]{1,0:T(8,128)(2,1)S(1)} collective-permute-done((bf16[768,1152]{1,0:T(8,128)(2,1)S(1)}, bf16[768,1152]{1,0:T(8,128)(2,1)S(1)}, u32[]{:S(2)}, u32[]{:S(2)}) %collective-permute-start.3) | collective-permute-done | bytes 1769504 | tf_op jit(solution)/shard_map/ppermute | solution.py:15
  276.3 2.0 divide_convert_fusion
  278.2 1.8 fusion.17
  280.1 0.0 collective-permute-done.7
  280.1 0.4 add.97
  280.5 0.3 collective-permute-start.8
  280.8 1.7 fusion.31
  282.5 1.8 convolution_add_fusion.4
  284.3 1.8 convolution_add_fusion.3
  286.0 1.8 convolution_add_fusion.2
  287.8 2.0 fusion.7
  289.8 1.9 fusion.10
  291.8 60.2 %collective-permute-done.8 = f32[768,1152]{1,0:T(8,128)S(1)} collective-permute-done((f32[768,1152]{1,0:T(8,128)S(1)}, f32[768,1152]{1,0:T(8,128)S(1)}, u32[]{:S(2)}, u32[]{:S(2)}) %collective-permute-start.8) | collective-permute-done | bytes 3538976 | tf_op jit(solution)/shard_map/ppermute | solution.py:15
  352.0 0.7 fusion.12
  352.7 2.0 fusion.15
  (2 shorter events, 0.0 us)
Async XLA Ops:
  0.6 2.0 copy-start
  2.7 2.1 copy-start.1
  8.7 66.5 %collective-permute-start.4 = (f32[768,1152]{1,0:T(8,128)S(1)}, f32[768,1152]{1,0:T(8,128)S(1)}, u32[]{:S(2)}, u32[]{:S(2)}) collective-permute-start(f32[768,1152]{1,0:T(8,128)S(1)} %fusion.24), channel_id=1, source_target_pairs={{31,0},{0,1},{1,2},{2,3},{3,4},{4,5},{5,6},{6,7},{7,8},{8,9},{9,10... | collective-permute-start | bytes 10616840 | tf_op jit(solution)/shard_map/ppermute | solution.py:15
  9.2 64.1 %collective-permute-start = (bf16[768,1152]{1,0:T(8,128)(2,1)S(1)}, bf16[768,1152]{1,0:T(8,128)(2,1)S(1)}, u32[]{:S(2)}, u32[]{:S(2)}) collective-permute-start(bf16[768,1152]{1,0:T(8,128)(2,1)S(1)} %fusion.2), channel_id=1, source_target_pairs={{31,0},{0,1},{1,2},{2,3},{3,4},{4,5},{5,6},{6,7},{7,8},{8,9},{9,10... | collective-permute-start | bytes 5308424 | tf_op jit(solution)/shard_map/ppermute | solution.py:15
  77.1 67.4 %collective-permute-start.5 = (f32[768,1152]{1,0:T(8,128)S(1)}, f32[768,1152]{1,0:T(8,128)S(1)}, u32[]{:S(2)}, u32[]{:S(2)}) collective-permute-start(f32[768,1152]{1,0:T(8,128)S(1)} %convolution_add_fusion), channel_id=1, source_target_pairs={{31,0},{0,1},{1,2},{2,3},{3,4},{4,5},{5,6},{6,7},{7,8},{8,9},{9,10... | collective-permute-start | bytes 10616840 | tf_op jit(solution)/shard_map/ppermute | solution.py:15
  77.2 63.5 %collective-permute-start.1 = (bf16[768,1152]{1,0:T(8,128)(2,1)S(1)}, bf16[768,1152]{1,0:T(8,128)(2,1)S(1)}, u32[]{:S(2)}, u32[]{:S(2)}) collective-permute-start(bf16[768,1152]{1,0:T(8,128)(2,1)S(1)} %collective-permute-done), channel_id=1, source_target_pairs={{31,0},{0,1},{1,2},{2,3},{3,4},{4,5},{5,6},{6,7},{7,8},{8,9},{9,10... | collective-permute-start | bytes 5308424 | tf_op jit(solution)/shard_map/ppermute | solution.py:15
  144.9 67.4 %collective-permute-start.6 = (f32[768,1152]{1,0:T(8,128)S(1)}, f32[768,1152]{1,0:T(8,128)S(1)}, u32[]{:S(2)}, u32[]{:S(2)}) collective-permute-start(f32[768,1152]{1,0:T(8,128)S(1)} %add.95), channel_id=1, source_target_pairs={{31,0},{0,1},{1,2},{2,3},{3,4},{4,5},{5,6},{6,7},{7,8},{8,9},{9,10... | collective-permute-start | bytes 10616840 | tf_op jit(solution)/shard_map/ppermute | solution.py:15
  145.0 63.5 %collective-permute-start.2 = (bf16[768,1152]{1,0:T(8,128)(2,1)S(1)}, bf16[768,1152]{1,0:T(8,128)(2,1)S(1)}, u32[]{:S(2)}, u32[]{:S(2)}) collective-permute-start(bf16[768,1152]{1,0:T(8,128)(2,1)S(1)} %collective-permute-done.1), channel_id=1, source_target_pairs={{31,0},{0,1},{1,2},{2,3},{3,4},{4,5},{5,6},{6,7},{7,8},{8,9},{9,10... | collective-permute-start | bytes 5308424 | tf_op jit(solution)/shard_map/ppermute | solution.py:15
  212.6 67.5 %collective-permute-start.7 = (f32[768,1152]{1,0:T(8,128)S(1)}, f32[768,1152]{1,0:T(8,128)S(1)}, u32[]{:S(2)}, u32[]{:S(2)}) collective-permute-start(f32[768,1152]{1,0:T(8,128)S(1)} %add.96), channel_id=1, source_target_pairs={{31,0},{0,1},{1,2},{2,3},{3,4},{4,5},{5,6},{6,7},{7,8},{8,9},{9,10... | collective-permute-start | bytes 10616840 | tf_op jit(solution)/shard_map/ppermute | solution.py:15
  212.7 63.6 %collective-permute-start.3 = (bf16[768,1152]{1,0:T(8,128)(2,1)S(1)}, bf16[768,1152]{1,0:T(8,128)(2,1)S(1)}, u32[]{:S(2)}, u32[]{:S(2)}) collective-permute-start(bf16[768,1152]{1,0:T(8,128)(2,1)S(1)} %collective-permute-done.2), channel_id=1, source_target_pairs={{31,0},{0,1},{1,2},{2,3},{3,4},{4,5},{5,6},{6,7},{7,8},{8,9},{9,10... | collective-permute-start | bytes 5308424 | tf_op jit(solution)/shard_map/ppermute | solution.py:15
  280.5 71.5 %collective-permute-start.8 = (f32[768,1152]{1,0:T(8,128)S(1)}, f32[768,1152]{1,0:T(8,128)S(1)}, u32[]{:S(2)}, u32[]{:S(2)}) collective-permute-start(f32[768,1152]{1,0:T(8,128)S(1)} %add.97), channel_id=1, source_target_pairs={{4,0},{5,1},{6,2},{7,3},{8,4},{9,5},{10,6},{11,7},{12,8},{13,9},{1... | collective-permute-start | bytes 10616840 | tf_op jit(solution)/shard_map/ppermute | solution.py:15
where the time goes:
time: 355 us
  waiting for transfers between devices  312 us (88%)
  matrix products  28.3 us (8%)
  other arithmetic  8.53 us (2%)
  starting transfers between devices  3.9 us (1%)
    ppermute x9, waiting for transfers between devices, from_behind(): return lax.ppermute(block, axis, route)  312 us
    dot_general x5, matrix products, tile_coef(): jnp.dot(image_block, text_block.T, preferred_element_type=jnp.float32)  9.91 us
    dot_general x5, matrix products, text_side(): lax.dot_general(coef, image_block, (((0,), (0,)), ((), ())), preferred_el...  9.35 us
    dot_general x5, matrix products, image_side(): return jnp.dot(coef, text_block, preferred_element_type=jnp.float32)  9.06 us
  transfers between devices with their start and end apart: 9, of which 5 were waited for; matrix products, arithmetic and copies ran while one was open for 7% of the time, Pallas kernels for 0%

commit v1 on v0

v1 whole, which is shorter than its diff:
```python
import functools

import jax
import jax.numpy as jnp
from jax import lax
from jax.experimental import pallas as pl
from jax.experimental.pallas import tpu as pltpu
from jax.sharding import PartitionSpec as P

EPS = 1e-06
CHUNKS = (512, 256)
ROW_TILE = 256
VMEM = pl.BlockSpec(memory_space=pltpu.VMEM)
SMEM = pl.BlockSpec(memory_space=pltpu.SMEM)
MIB = 1024 * 1024
LIMITS = {"own": 20, "mid": 26, "step": 20, "last": 20}
BLOCK = 1024
COSTS = {"own": 4, "mid": 0, "step": 4, "last": 4}
ANY = pl.BlockSpec(memory_space=pl.ANY)


def unit_rows(raw):
    wide = raw.astype(jnp.float32)
    inv = lax.rsqrt(jnp.sum(wide * wide, axis=-1, keepdims=True) + EPS)
    return wide * inv, inv


def hat_rows(raw):
    return unit_rows(raw)[0].astype(jnp.bfloat16)


def bands(refs):
    at = 0
    for ref in refs:
        for start in range(0, ref.shape[0], ROW_TILE):
            yield slice(at, at + ROW_TILE), ref, slice(start, start + ROW_TILE)
            at += ROW_TILE


def add_tile(total, base, own_hat, other, scale, bias, diagonal=False, block=None):
    rows, count = own_hat.shape[0], other.shape[0]
    if block is not None:
        block = min(block, count)
        add_tile(total, base, own_hat, other.at[:block], scale, bias)

        @pl.loop(1, count // block)
        def _(k):
            part = other.at[pl.ds(pl.multiple_of(k * block, block), block)]
            add_tile(total, total, own_hat, part, scale, bias)

        return
    for start in range(0, rows, ROW_TILE):
        band = slice(start, start + ROW_TILE)
        logits = lax.dot_general(
            own_hat[band, :], other[...], (((1,), (1,)), ((), ())),
            preferred_element_type=jnp.float32,
        )
        coef = jax.nn.sigmoid(scale * logits + bias)
        if diagonal:
            i = lax.broadcasted_iota(jnp.int32, coef.shape, 0) + start
            j = lax.broadcasted_iota(jnp.int32, coef.shape, 1)
            coef = coef - jnp.where(i == j, 1.0, 0.0)
        part = jnp.dot(coef.astype(jnp.bfloat16), other[...], preferred_element_type=jnp.float32)
        total[band, :] = part if base is None else base[band, :] + part


def project_band(grad, total, band, raw, scale):
    unit, inv = unit_rows(raw)
    acc = scale * total[band, :]
    along = jnp.sum(unit * acc, axis=-1, keepdims=True)
    grad[band, :] = (inv * (acc - unit * along)).astype(jnp.bfloat16)


def project_back(grad, total, raw, scale):
    for band, ref, part in bands(raw):
        project_band(grad, total, band, ref[part, :], scale)


def put_hat(hat, raw, at=0):
    rows = raw.shape[0]
    for start in range(0, rows, ROW_TILE):
        stop = min(start + ROW_TILE, rows)
        hat[at + start:at + stop, :] = hat_rows(raw[start:stop, :])


def own_kernel(scale_ref, bias_ref, *refs):
    n = len(CHUNKS)
    u, v, (u_hat, v_hat, u_total, v_total) = refs[0], refs[1:1 + n], refs[1 + n:]
    scale, bias = scale_ref[0], bias_ref[0]
    put_hat(u_hat, u)
    at = 0
    for part in v:
        put_hat(v_hat, part, at)
        at += part.shape[0]
    add_tile(u_total, None, u_hat, v_hat, scale, bias, True)
    add_tile(v_total, None, v_hat, u_hat, scale, bias, True)


def gather_hats(other, flag, take_far, at, plain, far_twins, twin):
    row = 0
    for block in plain:
        put_hat(other, block, row)
        row += block.shape[0]
    for far_twin in far_twins:
        size = far_twin.shape[0]
        for start in range(0, size, ROW_TILE):
            stop = min(start + ROW_TILE, size)
            extra = jnp.where(
                flag[0] == take_far, far_twin[start:stop, :], twin[at + start:at + stop, :]
            )
            other[row + start:row + stop, :] = hat_rows(extra)
        row, at = row + size, at + size


def step_kernel(take_far, at, count, far, scale_ref, bias_ref, flag, hat, base, *refs):
    plain, far_twins, (twin, total, other) = refs[:count], refs[count:count + far], refs[count + far:]
    gather_hats(other, flag, take_far, at, plain, far_twins, twin)
    add_tile(total, base, hat, other, scale_ref[0], bias_ref[0], block=BLOCK)


def mid_kernel(take_far, at, count, far, scale_ref, bias_ref, flag, hat, base, *refs):
    plain, far_twins, refs = refs[:count], refs[count:count + far], refs[count + far:]
    twin, raw, grad, total, other = refs
    gather_hats(other, flag, take_far, at, plain, far_twins, twin)
    add_tile(total, base, hat, other, scale_ref[0], bias_ref[0], block=BLOCK)
    project_back(grad, total, (raw,), scale_ref[0])


def last_kernel(take_far, at, count, far, scale_ref, bias_ref, flag, hat, base, *refs):
    n = len(CHUNKS)
    plain, far_twins, refs = refs[:count], refs[count:count + far], refs[count + far:]
    twin, raw, (done, image_grad, text_grad, total, other, grad, sems) = refs[0], refs[1:1 + n], refs[1 + n:]
    is_image = flag[1] == 0
    scale = scale_ref[0]
    whole = (
        pltpu.make_async_copy(done, text_grad, sems.at[0]),
        pltpu.make_async_copy(done, image_grad, sems.at[0]),
    )

    def each(pair, act):
        @pl.when(is_image)
        def _():
            act(pair[0])

        @pl.when(jnp.logical_not(is_image))
        def _():
            act(pair[1])

    each(whole, lambda copy: copy.start())
    gather_hats(other, flag, take_far, at, plain, far_twins, twin)
    add_tile(total, base, hat, other, scale, bias_ref[0], block=BLOCK)
    copies, row = [], 0
    for k, ref in enumerate(raw):
        band = slice(row, row + ref.shape[0])
        row += ref.shape[0]
        project_band(grad, total, band, ref[...], scale)
        copies.append((
            pltpu.make_async_copy(grad.at[band], image_grad.at[band], sems.at[1 + k]),
            pltpu.make_async_copy(grad.at[band], text_grad.at[band], sems.at[1 + k]),
        ))
        each(copies[-1], lambda copy: copy.start())
    for pair in (whole, *copies):
        each(pair, lambda copy: copy.wait())


def after(value, *before):
    return lax.optimization_barrier((value, *before))[0]


def shards(image, text, logit_scale, logit_bias):
    devices = lax.axis_size("batch")
    rows, width = image.shape
    me = lax.axis_index("batch")
    core, odd = lax.rem(me, 2), lax.rem(me // 2, 2)
    flag = jnp.stack([jnp.where(core == odd, 0, 1), odd]).astype(jnp.int32)

    def send(block, pairs):
        return lax.ppermute(block, "batch", pairs)

    def is_odd(i):
        return (i // 2) % 2 == 1

    over_x = [(i, i ^ 2) for i in range(devices)]
    out_y = [(i, (i + (4 if is_odd(i) else -4)) % devices) for i in range(devices)]
    back_y = [(i, (i + (-4 if is_odd(i) else 4)) % devices) for i in range(devices)]
    in_chip = [(i, i ^ 1) for i in range(devices)]

    even = odd == 0
    n = len(CHUNKS)
    spans = [slice(sum(CHUNKS[:k]), sum(CHUNKS[:k + 1])) for k in range(n)]
    u = jnp.where(even, text, image)
    v = [jnp.where(even, image[span], text[span]) for span in spans]

    def call(kind, body, outs, scratch, ins, products, out_spec=VMEM):
        specs = [SMEM, SMEM] + [SMEM if a.ndim == 1 else VMEM for a in ins]
        return pl.pallas_call(
            body,
            out_shape=outs,
            in_specs=specs,
            out_specs=jax.tree.map(lambda _: out_spec, outs),
            scratch_shapes=scratch,
            compiler_params=pltpu.CompilerParams(vmem_limit_bytes=LIMITS[kind] * MIB),
            cost_estimate=pl.CostEstimate(
                flops=COSTS[kind] * rows * width * products, bytes_accessed=0, transcendentals=0
            ),
        )(logit_scale, logit_bias, *ins)

    hat_type = jax.ShapeDtypeStruct((rows, width), jnp.bfloat16)
    sum_type = jax.ShapeDtypeStruct((rows, width), jnp.float32)
    running = pltpu.VMEM((rows, width), jnp.float32)

    def room(size):
        return pltpu.VMEM((size, width), jnp.bfloat16)

    def named(name, block, pairs):
        with jax.named_scope(name):
            return send(block, pairs)

    def step(kind, take_far, start, hat, base, plain, far_twins, extra=()):
        size = sum(block.shape[0] for block in (*plain, *far_twins))
        ins = (flag, hat, base, *plain, *far_twins, twin, *extra)
        body, out, scratch, spec = {
            "step": (step_kernel, sum_type, [room(size)], VMEM),
            "mid": (mid_kernel, hat_type, [running, room(size)], VMEM),
            "last": (
                last_kernel, (hat_type, hat_type),
                [running, room(size), room(rows), pltpu.SemaphoreType.DMA((1 + n,))], ANY,
            ),
        }[kind]
        body = functools.partial(body, take_far, start, len(plain), len(far_twins))
        return call(kind, body, out, scratch, ins, size, spec)

    p1x = named("p1x", u, over_x)
    p1y = [named(f"p1y{k}", v[k], out_y) for k in range(n)]
    u_own, *u_part = lax.optimization_barrier((u, *(u[span] for span in spans)))
    u_hat, v_hat, u_total, v_total = call(
        "own", own_kernel, (hat_type, hat_type, sum_type, sum_type), [], (u_own, *v), rows * 2
    )
    late_text, late_image, _ = lax.optimization_barrier((text, image, u))
    twin = named("twin", jnp.where(core == 0, late_text, late_image), in_chip)
    p1x, twin, v_hat, *p1y = lax.optimization_barrier((p1x, twin, v_hat, *p1y))
    p2x, p2y = [None] * n, [None] * n
    for k in range(n):
        p2x[k] = named(f"p2x{k}", p1y[k], over_x)
        p2y[k] = named(f"p2y{k}", after(u_part[k], p1y[k]), back_y)
    s1x = named("s1x", p1x, in_chip)
    s1y = [named(f"s1y{k}", p1y[k], in_chip) for k in range(n)]
    u_grad = token = step("mid", 1, 0, u_hat, u_total, [p1x, s1x, *p1y], s1y, (u_own,))
    for k in range(n):
        near_twin = named(f"s2x{k}", after(p2x[k], token), in_chip)
        far_twin = named(f"s2y{k}", after(p2y[k], token), in_chip)
        plain, start = [p2x[k], p2y[k], near_twin], spans[k].start
        if k < n - 1:
            v_total = token = step("step", 0, start, v_hat, v_total, plain, [far_twin])
        else:
            return step("last", 0, start, v_hat, v_total, plain, [far_twin], (*v, u_grad))


def solution(mesh):
    placed = (P("batch", None), P("batch", None), P(), P())
    return jax.shard_map(
        shards,
        mesh=mesh,
        in_specs=placed,
        out_specs=(P("batch", None), P("batch", None)),
        check_vma=False,
    )
```

time: 355 us -> 112 us (0.32)
  waiting for transfers between devices: 312 us -> 36.3 us
  Pallas kernels: 0 us -> 44.4 us
  matrix products: 28.3 us -> 0 us
  local copies, waits for them, and re-layouts: 0.01 us -> 12 us
  starting transfers between devices: 3.9 us -> 14.1 us
  other arithmetic: 8.53 us -> 2.29 us
    ppermute x9 -> x15, waiting for transfers between devices: 312 us -> 36.3 us  [send(): return lax.ppermute(block, 'batch', pairs)]
    pallas_call x0 -> x4, Pallas kernels: none -> 44.4 us  [call(): pl.pallas_call(body, out_shape=outs, in_specs=specs, out_specs=jax.tree.m...]
    dot_general x15 -> x0, matrix products: 28.3 us -> none  [the longest x5 9.91 us: tile_coef(): jnp.dot(image_block, text_block.T, preferred_element_type=jnp.float32)]
    ppermute x9 -> x15, starting transfers between devices: 3.9 us -> 14.1 us  [send(): return lax.ppermute(block, 'batch', pairs)]
    unnamed x4 -> x32, local copies, waits for them, and re-layouts: 0.01 us -> 10 us
    convert_element_type x3 -> x0, other arithmetic: 4.3 us -> none  [the longest x2 3.94 us: project_back(): return (inv * (acc - unit * along)).astype(jnp.bfloat16)]
  transfers between devices with their start and end apart: 9 -> 15, of which waited for: 5 -> 8; matrix products, arithmetic and copies ran while one was open for 7% -> 2% of each run, Pallas kernels for 0% -> 34%
where the time goes in v1:
time: 112 us; the launch traced here: 111 us
  Pallas kernels  44.4 us (40%)
  waiting for transfers between devices  36.3 us (32%)
  starting transfers between devices  14.1 us (13%)
  local copies, waits for them, and re-layouts  12 us (11%)
  other arithmetic  2.29 us (2%)
  between operations  2.27 us (2%)
    pallas_call x4, Pallas kernels, call(): pl.pallas_call(body, out_shape=outs, in_specs=specs, out_specs=jax.tree.m...  44.4 us
    ppermute x15, waiting for transfers between devices, send(): return lax.ppermute(block, 'batch', pairs)  36.3 us
    ppermute x15, starting transfers between devices, send(): return lax.ppermute(block, 'batch', pairs)  14.1 us
    unnamed x32, local copies, waits for them, and re-layouts  10 us
  transfers between devices with their start and end apart: 15, of which 8 were waited for; matrix products, arithmetic and copies ran while one was open for 2% of the time, Pallas kernels for 34%

profile of v1, /device:TPU:0, one launch (start us, length us, event | category | flops | bytes accessed | tf_op | source)
XLA Modules:
  0.0 111.4 jit_solution(16370849714439717993)
XLA Ops:
  0.7 0.0 copy-start.12
  0.7 1.8 %broadcast_select_fusion.1.refs_0_.refs_7_ = bf16[768,1152]{1,0:T(8,128)(2,1)S(1)} fusion(bf16[768,1152]{1,0:T(8,128)(2,1)} %param.5, bf16[768,1152]{1,0:T(8,128)(2,1)} %param.4, pred[]{:T(512)S(6)} %eq.10), kind=kLoop, calls=%fused_computation.1 | loop fusion | flops 884736 | bytes 5308417 | tf_op jit(solution)/shard_map/jit(_where)/select_n | solution.py:191
  2.5 3.0 %collective-permute-start = (bf16[768,1152]{1,0:T(8,128)(2,1)S(1)}, bf16[768,1152]{1,0:T(8,128)(2,1)}, u32[]{:S(2)}, u32[]{:S(2)}) collective-permute-start(bf16[768,1152]{1,0:T(8,128)(2,1)S(1)} %broadcast_select_fusion.1.refs_0_.refs_7_), channel_id=1, source_target_pairs={{0,2},{1,3},{2,0},{3,1},{4,6},{5,7},{6,4},{7,5},{8,10},{9,11},{10,... | collective-permute-start | bytes 5308424 | tf_op jit(solution)/shard_map/p1x/ppermute | solution.py:178
  5.5 0.0 copy-done.12
  5.5 0.0 copy-start.13
  5.5 0.0 copy-start.14
  5.5 0.2 broadcast_select_fusion
  5.7 1.2 %collective-permute-start.1 = (bf16[768,1152]{1,0:T(8,128)(2,1)S(1)}, bf16[768,1152]{1,0:T(8,128)(2,1)S(1)}, u32[]{:S(2)}, u32[]{:S(2)}) collective-permute-start(bf16[768,1152]{1,0:T(8,128)(2,1)S(1)} %broadcast_select_fusion), channel_id=1, source_target_pairs={{0,1},{1,0},{2,3},{3,2},{4,5},{5,4},{6,7},{7,6},{8,9},{9,8},{10,11... | collective-permute-start | bytes 5308424 | tf_op jit(solution)/shard_map/twin/ppermute | solution.py:178
  6.9 0.0 copy-done.13
  7.0 0.5 copy-done.14
  7.5 0.1 slice_select_fusion.refs_1_.refs_5_
  7.6 0.0 copy-start.4
  7.6 4.6 %collective-permute-start.2 = (bf16[512,1152]{1,0:T(8,128)(2,1)S(1)}, bf16[512,1152]{1,0:T(8,128)(2,1)}, u32[]{:S(2)}, u32[]{:S(2)}) collective-permute-start(bf16[512,1152]{1,0:T(8,128)(2,1)S(1)} %slice_select_fusion.refs_1_.refs_5_), channel_id=1, source_target_pairs={{0,28},{1,29},{2,6},{3,7},{4,0},{5,1},{6,10},{7,11},{8,4},{9,5},{1... | collective-permute-start | bytes 3538952 | tf_op jit(solution)/shard_map/p1y0/ppermute | solution.py:178
  12.3 0.1 slice_select_fusion.1.refs_2_.refs_6_
  12.3 0.0 copy-start.6
  12.3 0.6 collective-permute-start.3
  12.9 1.1 slice.24
  14.0 0.9 slice.25
  16.2 0.0 copy-done.4
  16.2 0.0 copy-done.6
  16.2 7.0 %shard_map.59 = (bf16[768,1152]{1,0:T(8,128)(2,1)S(1)}, bf16[768,1152]{1,0:T(8,128)(2,1)S(1)}, f32[768,1152]{1,0:T(8,128)S(1)}, f32[768,1152]{1,0:T(8,128)S(1)}) custom-call(f32[1]{0:T(128)S(6)} %copy.6.scale_ref, f32[1]{0:T(128)S(6)} %copy.7.bias_ref, bf16[768,1152]{1,0:T(8,128)(2,1)S(1)} %broadcast_select_fusion.1.refs_0_.refs_7_, ...), custom_call_target="tpu_custom_call" | custom-call | flops 5435817984 | tf_op jit(solution)/shard_map/pallas_call | solution.py:196
  23.3 0.0 copy-start
  23.3 1.8 %copy-done = f32[768,1152]{1,0:T(8,128)} copy-done((f32[768,1152]{1,0:T(8,128)}, f32[768,1152]{1,0:T(8,128)S(1)}, u32[]{:S(2)}) %copy-start) | copy-done | bytes 3538968
  25.1 0.0 copy-start.2
  25.1 1.2 %copy-done.2 = bf16[768,1152]{1,0:T(8,128)(2,1)} copy-done((bf16[768,1152]{1,0:T(8,128)(2,1)}, bf16[768,1152]{1,0:T(8,128)(2,1)S(1)}, u32[]{:S(2)}) %copy-start.2) | copy-done | bytes 1769496
  26.3 1.2 %copy-done.8 = bf16[768,1152]{1,0:T(8,128)(2,1)} copy-done((bf16[768,1152]{1,0:T(8,128)(2,1)}, bf16[768,1152]{1,0:T(8,128)(2,1)S(1)}, u32[]{:S(2)}) %copy-start.8) | copy-done | bytes 1769496
  27.5 1.7 %copy-done.10 = f32[768,1152]{1,0:T(8,128)} copy-done((f32[768,1152]{1,0:T(8,128)}, f32[768,1152]{1,0:T(8,128)S(1)}, u32[]{:S(2)}) %copy-start.10) | copy-done | bytes 3538968
  29.2 21.1 %collective-permute-done.3.refs_3_ = bf16[256,1152]{1,0:T(8,128)(2,1)} collective-permute-done((bf16[256,1152]{1,0:T(8,128)(2,1)S(1)}, bf16[256,1152]{1,0:T(8,128)(2,1)}, u32[]{:S(2)}, u32[]{:S(2)}) %collective-permute-start.3) | collective-permute-done | bytes 589856 | tf_op jit(solution)/shard_map/p1y1/ppermute | solution.py:178
  50.4 0.0 collective-permute-done.2.refs_2_
  50.4 0.0 collective-permute-done.1.refs_6_.refs_4_
  50.4 0.0 collective-permute-done.refs_0_
  50.4 0.1 collective-permute-start.6
  50.5 0.5 collective-permute-start.7
  51.0 0.4 collective-permute-start.5
  51.4 2.7 %collective-permute-start.4 = (bf16[512,1152]{1,0:T(8,128)(2,1)}, bf16[512,1152]{1,0:T(8,128)(2,1)}, u32[]{:S(2)}, u32[]{:S(2)}) collective-permute-start(bf16[512,1152]{1,0:T(8,128)(2,1)} %collective-permute-done.2.refs_2_), channel_id=1, source_target_pairs={{0,2},{1,3},{2,0},{3,1},{4,6},{5,7},{6,4},{7,5},{8,10},{9,11},{10,... | collective-permute-start | bytes 3538952 | tf_op jit(solution)/shard_map/p2x0/ppermute | solution.py:178
  54.1 0.0 collective-permute-start.8
  54.1 0.1 pad_add_fusion.flag
  54.2 2.9 %collective-permute-done.8.refs_5_ = bf16[256,1152]{1,0:T(8,128)(2,1)} collective-permute-done((bf16[256,1152]{1,0:T(8,128)(2,1)}, bf16[256,1152]{1,0:T(8,128)(2,1)}, u32[]{:S(2)}, u32[]{:S(2)}) %collective-permute-start.8) | collective-permute-done | bytes 589856 | tf_op jit(solution)/shard_map/s1y1/ppermute | solution.py:178
  57.0 0.0 collective-permute-done.7.refs_4_
  57.0 0.0 collective-permute-done.6.refs_1_
  57.0 2.0 %copy-done.1 = f32[768,1152]{1,0:T(8,128)S(1)} copy-done((f32[768,1152]{1,0:T(8,128)S(1)}, f32[768,1152]{1,0:T(8,128)}, u32[]{:S(2)}) %copy-start.1) | copy-done | bytes 3538968
  59.0 1.5 %copy-done.3 = bf16[768,1152]{1,0:T(8,128)(2,1)S(1)} copy-done((bf16[768,1152]{1,0:T(8,128)(2,1)S(1)}, bf16[768,1152]{1,0:T(8,128)(2,1)}, u32[]{:S(2)}) %copy-start.3) | copy-done | bytes 1769496
  60.5 19.2 %shard_map.60.refs_7_ = bf16[768,1152]{1,0:T(8,128)(2,1)S(1)} custom-call(f32[1]{0:T(128)S(6)} %copy.6.scale_ref, f32[1]{0:T(128)S(6)} %copy.7.bias_ref, s32[2]{0:T(128)S(1)} %pad_add_fusion.flag, bf16[768,1152]{1,0:T(8,128)(2,1)S(1)} %copy-done.3, f32[768,1152]{1,0:T(8,128)S(1)} %copy-done.1, bf16[768,1152]{1,0:T(8,128)(2,1)} %collective-permute-done.refs_0_, ...), custom_call_target="tpu_custom_call" | custom-call | tf_op jit(solution)/shard_map/pallas_call | solution.py:196
  79.8 3.0 %collective-permute-done.5.refs_1_ = bf16[512,1152]{1,0:T(8,128)(2,1)} collective-permute-done((bf16[512,1152]{1,0:T(8,128)(2,1)}, bf16[512,1152]{1,0:T(8,128)(2,1)}, u32[]{:S(2)}, u32[]{:S(2)}) %collective-permute-start.5) | collective-permute-done | bytes 1179680 | tf_op jit(solution)/shard_map/p2y0/ppermute | solution.py:178
  82.8 0.0 collective-permute-start.10
  82.8 0.0 collective-permute-done.4.refs_0_
  82.8 0.5 collective-permute-start.9
  83.3 0.0 collective-permute-start.11
  83.3 0.0 copy-done.15
  83.3 0.0 collective-permute-start.12
  83.3 2.5 %collective-permute-done.10.refs_3_ = bf16[512,1152]{1,0:T(8,128)(2,1)S(1)} collective-permute-done((bf16[512,1152]{1,0:T(8,128)(2,1)}, bf16[512,1152]{1,0:T(8,128)(2,1)S(1)}, u32[]{:S(2)}, u32[]{:S(2)}) %collective-permute-start.10) | collective-permute-done | bytes 1179680 | tf_op jit(solution)/shard_map/s2y0/ppermute | solution.py:178
  85.8 1.7 %collective-permute-done.9.refs_2_ = bf16[512,1152]{1,0:T(8,128)(2,1)S(1)} collective-permute-done((bf16[512,1152]{1,0:T(8,128)(2,1)}, bf16[512,1152]{1,0:T(8,128)(2,1)S(1)}, u32[]{:S(2)}, u32[]{:S(2)}) %collective-permute-start.9) | collective-permute-done | bytes 1179680 | tf_op jit(solution)/shard_map/s2x0/ppermute | solution.py:178
  87.5 0.0 copy-done.9
  87.5 0.0 copy-done.11
  87.5 11.3 %shard_map.61.base = f32[768,1152]{1,0:T(8,128)S(1)} custom-call(f32[1]{0:T(128)S(6)} %copy.6.scale_ref, f32[1]{0:T(128)S(6)} %copy.7.bias_ref, s32[2]{0:T(128)S(1)} %pad_add_fusion.flag, bf16[768,1152]{1,0:T(8,128)(2,1)S(1)} %copy-done.9, f32[768,1152]{1,0:T(8,128)S(1)} %copy-done.11, bf16[512,1152]{1,0:T(8,128)(2,1)} %collective-permute-done.4.refs_0_, ...), custom_call_target="tpu_custom_call" | custom-call | flops 7247757312 | tf_op jit(solution)/shard_map/pallas_call | solution.py:196
  98.8 2.7 %collective-permute-done.12.refs_1_ = bf16[256,1152]{1,0:T(8,128)(2,1)S(1)} collective-permute-done((bf16[256,1152]{1,0:T(8,128)(2,1)S(1)}, bf16[256,1152]{1,0:T(8,128)(2,1)S(1)}, u32[]{:S(2)}, u32[]{:S(2)}) %collective-permute-start.12) | collective-permute-done | bytes 589856 | tf_op jit(solution)/shard_map/p2y1/ppermute | solution.py:178
  101.5 0.0 collective-permute-start.14
  101.5 0.0 collective-permute-done.11.refs_0_
  101.5 0.5 collective-permute-start.13
  102.0 1.5 %collective-permute-done.14.refs_3_ = bf16[256,1152]{1,0:T(8,128)(2,1)S(1)} collective-permute-done((bf16[256,1152]{1,0:T(8,128)(2,1)S(1)}, bf16[256,1152]{1,0:T(8,128)(2,1)S(1)}, u32[]{:S(2)}, u32[]{:S(2)}) %collective-permute-start.14) | collective-permute-done | bytes 589856 | tf_op jit(solution)/shard_map/s2y1/ppermute | solution.py:178
  103.5 0.8 collective-permute-done.13.refs_2_
  104.4 0.0 copy-done.5
  104.4 0.0 copy-done.7
  104.4 6.9 %shard_map.62 = (bf16[768,1152]{1,0:T(8,128)(2,1)}, bf16[768,1152]{1,0:T(8,128)(2,1)}) custom-call(f32[1]{0:T(128)S(6)} %copy.6.scale_ref, f32[1]{0:T(128)S(6)} %copy.7.bias_ref, s32[2]{0:T(128)S(1)} %pad_add_fusion.flag, bf16[768,1152]{1,0:T(8,128)(2,1)S(1)} %copy-done.9, f32[768,1152]{1,0:T(8,128)S(1)} %shard_map.61.base, ...), custom_call_target="tpu_custom_call" | custom-call | flops 3623878656 | tf_op jit(solution)/shard_map/pallas_call | solution.py:196
  (9 shorter events, 0.0 us)
Async XLA Ops:
  0.7 4.8 %copy-start.12 = (bf16[768,1152]{1,0:T(8,128)(2,1)S(1)}, bf16[768,1152]{1,0:T(8,128)(2,1)}, u32[]{:S(2)}) copy-start(bf16[768,1152]{1,0:T(8,128)(2,1)} %param.5) | copy-start | bytes 5308420
  2.5 47.9 %collective-permute-start = (bf16[768,1152]{1,0:T(8,128)(2,1)S(1)}, bf16[768,1152]{1,0:T(8,128)(2,1)}, u32[]{:S(2)}, u32[]{:S(2)}) collective-permute-start(bf16[768,1152]{1,0:T(8,128)(2,1)S(1)} %broadcast_select_fusion.1.refs_0_.refs_7_), channel_id=1, source_target_pairs={{0,2},{1,3},{2,0},{3,1},{4,6},{5,7},{6,4},{7,5},{8,10},{9,11},{10,... | collective-permute-start | bytes 5308424 | tf_op jit(solution)/shard_map/p1x/ppermute | solution.py:178
  5.5 1.5 %copy-start.13 = (bf16[768,1152]{1,0:T(8,128)(2,1)S(1)}, bf16[768,1152]{1,0:T(8,128)(2,1)}, u32[]{:S(2)}) copy-start(bf16[768,1152]{1,0:T(8,128)(2,1)} %param.5) | copy-start | bytes 5308420
  5.5 2.0 %copy-start.14 = (bf16[768,1152]{1,0:T(8,128)(2,1)S(1)}, bf16[768,1152]{1,0:T(8,128)(2,1)}, u32[]{:S(2)}) copy-start(bf16[768,1152]{1,0:T(8,128)(2,1)} %param.4) | copy-start | bytes 5308420
  5.7 44.7 %collective-permute-start.1 = (bf16[768,1152]{1,0:T(8,128)(2,1)S(1)}, bf16[768,1152]{1,0:T(8,128)(2,1)S(1)}, u32[]{:S(2)}, u32[]{:S(2)}) collective-permute-start(bf16[768,1152]{1,0:T(8,128)(2,1)S(1)} %broadcast_select_fusion), channel_id=1, source_target_pairs={{0,1},{1,0},{2,3},{3,2},{4,5},{5,4},{6,7},{7,6},{8,9},{9,8},{10,11... | collective-permute-start | bytes 5308424 | tf_op jit(solution)/shard_map/twin/ppermute | solution.py:178
  7.6 8.6 %copy-start.4 = (bf16[512,1152]{1,0:T(8,128)(2,1)}, bf16[512,1152]{1,0:T(8,128)(2,1)S(1)}, u32[]{:S(2)}) copy-start(bf16[512,1152]{1,0:T(8,128)(2,1)S(1)} %slice_select_fusion.refs_1_.refs_5_) | copy-start | bytes 3538948
  7.6 42.7 %collective-permute-start.2 = (bf16[512,1152]{1,0:T(8,128)(2,1)S(1)}, bf16[512,1152]{1,0:T(8,128)(2,1)}, u32[]{:S(2)}, u32[]{:S(2)}) collective-permute-start(bf16[512,1152]{1,0:T(8,128)(2,1)S(1)} %slice_select_fusion.refs_1_.refs_5_), channel_id=1, source_target_pairs={{0,28},{1,29},{2,6},{3,7},{4,0},{5,1},{6,10},{7,11},{8,4},{9,5},{1... | collective-permute-start | bytes 3538952 | tf_op jit(solution)/shard_map/p1y0/ppermute | solution.py:178
  12.3 3.9 %copy-start.6 = (bf16[256,1152]{1,0:T(8,128)(2,1)}, bf16[256,1152]{1,0:T(8,128)(2,1)S(1)}, u32[]{:S(2)}) copy-start(bf16[256,1152]{1,0:T(8,128)(2,1)S(1)} %slice_select_fusion.1.refs_2_.refs_6_) | copy-start | bytes 1769476
  12.3 38.0 %collective-permute-start.3 = (bf16[256,1152]{1,0:T(8,128)(2,1)S(1)}, bf16[256,1152]{1,0:T(8,128)(2,1)}, u32[]{:S(2)}, u32[]{:S(2)}) collective-permute-start(bf16[256,1152]{1,0:T(8,128)(2,1)S(1)} %slice_select_fusion.1.refs_2_.refs_6_), channel_id=1, source_target_pairs={{0,28},{1,29},{2,6},{3,7},{4,0},{5,1},{6,10},{7,11},{8,4},{9,5},{1... | collective-permute-start | bytes 1769480 | tf_op jit(solution)/shard_map/p1y1/ppermute | solution.py:178
  23.3 1.8 %copy-start = (f32[768,1152]{1,0:T(8,128)}, f32[768,1152]{1,0:T(8,128)S(1)}, u32[]{:S(2)}) copy-start(f32[768,1152]{1,0:T(8,128)S(1)} %get-tuple-element.32.base) | copy-start | bytes 10616836
  25.1 1.2 %copy-start.2 = (bf16[768,1152]{1,0:T(8,128)(2,1)}, bf16[768,1152]{1,0:T(8,128)(2,1)S(1)}, u32[]{:S(2)}) copy-start(bf16[768,1152]{1,0:T(8,128)(2,1)S(1)} %get-tuple-element.31.hat) | copy-start | bytes 5308420
  26.3 1.2 %copy-start.8 = (bf16[768,1152]{1,0:T(8,128)(2,1)}, bf16[768,1152]{1,0:T(8,128)(2,1)S(1)}, u32[]{:S(2)}) copy-start(bf16[768,1152]{1,0:T(8,128)(2,1)S(1)} %get-tuple-element.26.hat) | copy-start | bytes 5308420
  27.5 1.8 %copy-start.10 = (f32[768,1152]{1,0:T(8,128)}, f32[768,1152]{1,0:T(8,128)S(1)}, u32[]{:S(2)}) copy-start(f32[768,1152]{1,0:T(8,128)S(1)} %get-tuple-element.27.base) | copy-start | bytes 10616836
  50.4 6.6 %collective-permute-start.6 = (bf16[768,1152]{1,0:T(8,128)(2,1)}, bf16[768,1152]{1,0:T(8,128)(2,1)}, u32[]{:S(2)}, u32[]{:S(2)}) collective-permute-start(bf16[768,1152]{1,0:T(8,128)(2,1)} %collective-permute-done.refs_0_), channel_id=1, source_target_pairs={{0,1},{1,0},{2,3},{3,2},{4,5},{5,4},{6,7},{7,6},{8,9},{9,8},{10,11... | collective-permute-start | bytes 5308424 | tf_op jit(solution)/shard_map/s1x/ppermute | solution.py:178
  50.5 6.6 %collective-permute-start.7 = (bf16[512,1152]{1,0:T(8,128)(2,1)}, bf16[512,1152]{1,0:T(8,128)(2,1)}, u32[]{:S(2)}, u32[]{:S(2)}) collective-permute-start(bf16[512,1152]{1,0:T(8,128)(2,1)} %collective-permute-done.2.refs_2_), channel_id=1, source_target_pairs={{0,1},{1,0},{2,3},{3,2},{4,5},{5,4},{6,7},{7,6},{8,9},{9,8},{10,11... | collective-permute-start | bytes 3538952 | tf_op jit(solution)/shard_map/s1y0/ppermute | solution.py:178
  51.0 31.8 %collective-permute-start.5 = (bf16[512,1152]{1,0:T(8,128)(2,1)}, bf16[512,1152]{1,0:T(8,128)(2,1)}, u32[]{:S(2)}, u32[]{:S(2)}) collective-permute-start(bf16[512,1152]{1,0:T(8,128)(2,1)} %slice.24), channel_id=1, source_target_pairs={{0,4},{1,5},{2,30},{3,31},{4,8},{5,9},{6,2},{7,3},{8,12},{9,13},{1... | collective-permute-start | bytes 3538952 | tf_op jit(solution)/shard_map/p2y0/ppermute | solution.py:178
  51.4 31.4 %collective-permute-start.4 = (bf16[512,1152]{1,0:T(8,128)(2,1)}, bf16[512,1152]{1,0:T(8,128)(2,1)}, u32[]{:S(2)}, u32[]{:S(2)}) collective-permute-start(bf16[512,1152]{1,0:T(8,128)(2,1)} %collective-permute-done.2.refs_2_), channel_id=1, source_target_pairs={{0,2},{1,3},{2,0},{3,1},{4,6},{5,7},{6,4},{7,5},{8,10},{9,11},{10,... | collective-permute-start | bytes 3538952 | tf_op jit(solution)/shard_map/p2x0/ppermute | solution.py:178
  54.1 2.9 %collective-permute-start.8 = (bf16[256,1152]{1,0:T(8,128)(2,1)}, bf16[256,1152]{1,0:T(8,128)(2,1)}, u32[]{:S(2)}, u32[]{:S(2)}) collective-permute-start(bf16[256,1152]{1,0:T(8,128)(2,1)} %collective-permute-done.3.refs_3_), channel_id=1, source_target_pairs={{0,1},{1,0},{2,3},{3,2},{4,5},{5,4},{6,7},{7,6},{8,9},{9,8},{10,11... | collective-permute-start | bytes 1769480 | tf_op jit(solution)/shard_map/s1y1/ppermute | solution.py:178
  57.0 2.0 %copy-start.1 = (f32[768,1152]{1,0:T(8,128)S(1)}, f32[768,1152]{1,0:T(8,128)}, u32[]{:S(2)}) copy-start(f32[768,1152]{1,0:T(8,128)} %copy-done) | copy-start | bytes 10616836
  59.0 1.5 %copy-start.3 = (bf16[768,1152]{1,0:T(8,128)(2,1)S(1)}, bf16[768,1152]{1,0:T(8,128)(2,1)}, u32[]{:S(2)}) copy-start(bf16[768,1152]{1,0:T(8,128)(2,1)} %copy-done.2) | copy-start | bytes 5308420
  60.5 22.8 %copy-start.15 = (bf16[256,1152]{1,0:T(8,128)(2,1)S(1)}, bf16[256,1152]{1,0:T(8,128)(2,1)}, u32[]{:S(2)}) copy-start(bf16[256,1152]{1,0:T(8,128)(2,1)} %slice.25) | copy-start | bytes 1769476
  60.5 27.0 %copy-start.9 = (bf16[768,1152]{1,0:T(8,128)(2,1)S(1)}, bf16[768,1152]{1,0:T(8,128)(2,1)}, u32[]{:S(2)}) copy-start(bf16[768,1152]{1,0:T(8,128)(2,1)} %copy-done.8) | copy-start | bytes 5308420
  60.5 27.0 %copy-start.11 = (f32[768,1152]{1,0:T(8,128)S(1)}, f32[768,1152]{1,0:T(8,128)}, u32[]{:S(2)}) copy-start(f32[768,1152]{1,0:T(8,128)} %copy-done.10) | copy-start | bytes 10616836
  82.8 3.1 %collective-permute-start.10 = (bf16[512,1152]{1,0:T(8,128)(2,1)}, bf16[512,1152]{1,0:T(8,128)(2,1)S(1)}, u32[]{:S(2)}, u32[]{:S(2)}) collective-permute-start(bf16[512,1152]{1,0:T(8,128)(2,1)} %collective-permute-done.5.refs_1_), channel_id=1, source_target_pairs={{0,1},{1,0},{2,3},{3,2},{4,5},{5,4},{6,7},{7,6},{8,9},{9,8},{10,11... | collective-permute-start | bytes 3538952 | tf_op jit(solution)/shard_map/s2y0/ppermute | solution.py:178
  82.8 4.7 %collective-permute-start.9 = (bf16[512,1152]{1,0:T(8,128)(2,1)}, bf16[512,1152]{1,0:T(8,128)(2,1)S(1)}, u32[]{:S(2)}, u32[]{:S(2)}) collective-permute-start(bf16[512,1152]{1,0:T(8,128)(2,1)} %collective-permute-done.4.refs_0_), channel_id=1, source_target_pairs={{0,1},{1,0},{2,3},{3,2},{4,5},{5,4},{6,7},{7,6},{8,9},{9,8},{10,11... | collective-permute-start | bytes 3538952 | tf_op jit(solution)/shard_map/s2x0/ppermute | solution.py:178
  83.3 18.2 %collective-permute-start.11 = (bf16[256,1152]{1,0:T(8,128)(2,1)}, bf16[256,1152]{1,0:T(8,128)(2,1)S(1)}, u32[]{:S(2)}, u32[]{:S(2)}) collective-permute-start(bf16[256,1152]{1,0:T(8,128)(2,1)} %collective-permute-done.3.refs_3_), channel_id=1, source_target_pairs={{0,2},{1,3},{2,0},{3,1},{4,6},{5,7},{6,4},{7,5},{8,10},{9,11},{10,... | collective-permute-start | bytes 1769480 | tf_op jit(solution)/shard_map/p2x1/ppermute | solution.py:178
  83.3 18.2 %collective-permute-start.12 = (bf16[256,1152]{1,0:T(8,128)(2,1)S(1)}, bf16[256,1152]{1,0:T(8,128)(2,1)S(1)}, u32[]{:S(2)}, u32[]{:S(2)}) collective-permute-start(bf16[256,1152]{1,0:T(8,128)(2,1)S(1)} %copy-done.15), channel_id=1, source_target_pairs={{0,4},{1,5},{2,30},{3,31},{4,8},{5,9},{6,2},{7,3},{8,12},{9,13},{1... | collective-permute-start | bytes 1769480 | tf_op jit(solution)/shard_map/p2y1/ppermute | solution.py:178
  87.5 16.8 %copy-start.5 = (bf16[512,1152]{1,0:T(8,128)(2,1)S(1)}, bf16[512,1152]{1,0:T(8,128)(2,1)}, u32[]{:S(2)}) copy-start(bf16[512,1152]{1,0:T(8,128)(2,1)} %copy-done.4) | copy-start | bytes 3538948
  87.5 16.8 %copy-start.7 = (bf16[256,1152]{1,0:T(8,128)(2,1)S(1)}, bf16[256,1152]{1,0:T(8,128)(2,1)}, u32[]{:S(2)}) copy-start(bf16[256,1152]{1,0:T(8,128)(2,1)} %copy-done.6) | copy-start | bytes 1769476
  101.5 2.0 %collective-permute-start.14 = (bf16[256,1152]{1,0:T(8,128)(2,1)S(1)}, bf16[256,1152]{1,0:T(8,128)(2,1)S(1)}, u32[]{:S(2)}, u32[]{:S(2)}) collective-permute-start(bf16[256,1152]{1,0:T(8,128)(2,1)S(1)} %collective-permute-done.12.refs_1_), channel_id=1, source_target_pairs={{0,1},{1,0},{2,3},{3,2},{4,5},{5,4},{6,7},{7,6},{8,9},{9,8},{10,11... | collective-permute-start | bytes 1769480 | tf_op jit(solution)/shard_map/s2y1/ppermute | solution.py:178
  101.5 2.8 %collective-permute-start.13 = (bf16[256,1152]{1,0:T(8,128)(2,1)S(1)}, bf16[256,1152]{1,0:T(8,128)(2,1)S(1)}, u32[]{:S(2)}, u32[]{:S(2)}) collective-permute-start(bf16[256,1152]{1,0:T(8,128)(2,1)S(1)} %collective-permute-done.11.refs_0_), channel_id=1, source_target_pairs={{0,1},{1,0},{2,3},{3,2},{4,5},{5,4},{6,7},{7,6},{8,9},{9,8},{10,11... | collective-permute-start | bytes 1769480 | tf_op jit(solution)/shard_map/s2x1/ppermute | solution.py:178
